TPU v7x, 128 devices: a whole 4x4x4 slice. The times are simulated.
128 devices in a mesh: grid: 32 (over y, x, z_lo), mode: 4 (over z_hi, core).
Axes of the slice: x: 4, y: 4, z: 4 (z_hi: 2, z_lo: 2; z = z_hi * 2 + z_lo), core: 2. Of those that a mesh axis runs over, the one named last changes fastest.
Arguments:
- held_modes: bfloat16 [224, 3, 128, 4, 128], P('mode', None, 'grid'), may hold values from -6 to 6
- new_modes: bfloat16 [32, 3, 128, 4, 128], P('mode', None, 'grid'), may hold values from -6 to 6
Outputs:
- new_third: float32 [256, 8192], P('grid', 'mode')
- held_third_new_first: float32 [256, 7168], P('grid', 'mode')
- held_third_new_second: float32 [224, 7168], P('grid', 'mode')
All inputs are finite; a program needn't handle non-finite values.
Results may differ from a plain program's by a relative error of at most 0.0042.
Values may be sent and summed in bfloat16 or wider, within the bound.
A program may use at most 128 MiB of HBM per device.

v0:
```python
import math

import jax
import jax.numpy as jnp
from jax import lax
from jax.sharding import PartitionSpec as P


def with_halo(cells, sides, width):
    for axis, dim in sides:
        count = lax.axis_size(axis)
        head = lax.slice_in_dim(cells, 0, width, axis=dim)
        tail = lax.slice_in_dim(cells, cells.shape[dim] - width, cells.shape[dim], axis=dim)
        cells = jnp.concatenate(
            [
                lax.ppermute(tail, axis, [(i, (i + 1) % count) for i in range(count)]),
                cells,
                lax.ppermute(head, axis, [((i + 1) % count, i) for i in range(count)]),
            ],
            axis=dim,
        )
    return cells


def gradients(padded, own):
    wide = padded.astype(jnp.float32)
    centre = own.astype(jnp.float32)
    along_x = (wide[:, :, 2:] - wide[:, :, :-2]) * 0.5
    along_y = (jnp.roll(centre, -1, 3) - jnp.roll(centre, 1, 3)) * 0.5
    along_z = (jnp.roll(centre, -1, 4) - jnp.roll(centre, 1, 4)) * 0.5
    return jnp.stack([along_x, along_y, along_z], axis=2).astype(jnp.bfloat16)


def advect(velocity, grad_block):
    first = velocity[None, :, None, 0].astype(jnp.float32) * grad_block[:, None, :, 0].astype(
        jnp.float32
    )
    second = velocity[None, :, None, 1].astype(jnp.float32) * grad_block[:, None, :, 1].astype(
        jnp.float32
    )
    third = velocity[None, :, None, 2].astype(jnp.float32) * grad_block[:, None, :, 2].astype(
        jnp.float32
    )
    return (first + second + third).astype(jnp.bfloat16)


def contract(left, right):
    return lax.dot_general(
        left, right, (((1,), (1,)), ((), ())), preferred_element_type=jnp.float32
    )


def per_device(held_modes, new_modes):
    held_own = held_modes.shape[0]
    new_own = new_modes.shape[0]
    cell_count = held_modes.shape[2] * held_modes.shape[3] * held_modes.shape[4]
    weighting = 1.0 / math.sqrt(cell_count * lax.axis_size("grid"))
    own = jnp.concatenate([held_modes, new_modes], 0)
    padded = with_halo(own, (("grid", 2),), 1)
    slopes = gradients(padded, own).reshape(held_own + new_own, 3, 3, cell_count)
    held_all, new_all = (
        lax.all_gather(held_modes, "mode", axis=0, tiled=True),
        lax.all_gather(new_modes, "mode", axis=0, tiled=True),
    )
    held_count = held_all.shape[0]
    new_count = new_all.shape[0]
    total = held_count + new_count
    held_vel = held_all.reshape(held_count, 3, cell_count)
    new_vel = new_all.reshape(new_count, 3, cell_count)
    all_vel = jnp.concatenate([held_vel, new_vel], 0)
    all_flat = all_vel.reshape(total, 3 * cell_count)
    new_flat = new_vel.reshape(new_count, 3 * cell_count)
    width = 4
    new_slopes = slopes[held_own:].reshape(new_own // width, width, 3, 3, cell_count)
    held_slopes = slopes[:held_own].reshape(held_own // width, width, 3, 3, cell_count)

    def new_step(carry, grad_block):
        advected = advect(all_vel, grad_block).reshape(width * total, 3 * cell_count)
        return (carry, contract(all_flat, advected) * weighting)

    _, new_stack = lax.scan(new_step, jnp.zeros((), jnp.float32), new_slopes)
    new_terms = new_stack.transpose(1, 0, 2).reshape(total, new_own * total)

    def held_step(carry, grad_block):
        adv_new = advect(new_vel, grad_block).reshape(width * new_count, 3 * cell_count)
        adv_held = advect(held_vel, grad_block).reshape(width * held_count, 3 * cell_count)
        onto_all = (contract(all_flat, adv_new) * weighting).reshape(total, width, new_count)
        onto_new = (contract(adv_held, new_flat) * weighting).reshape(width, held_count, new_count)
        rows_held = onto_all[:held_count]
        rows_every = jnp.concatenate(
            [onto_new.transpose(1, 0, 2), onto_all[held_count:].transpose(2, 1, 0)], 0
        )
        return (carry, (rows_held, rows_every))

    _, (held_stack, every_stack) = lax.scan(held_step, jnp.zeros((), jnp.float32), held_slopes)
    terms_second = held_stack.transpose(1, 0, 2, 3).reshape(held_count, held_own * new_count)
    terms_first = every_stack.transpose(1, 0, 2, 3).reshape(total, held_own * new_count)
    new_third, out_first, out_second = (
        lax.psum_scatter(new_terms, "grid", scatter_dimension=0, tiled=True),
        lax.psum_scatter(terms_first, "grid", scatter_dimension=0, tiled=True),
        lax.psum_scatter(terms_second, "grid", scatter_dimension=0, tiled=True),
    )
    return (new_third, out_first, out_second)


def solution(mesh):
    placed = (P("mode", None, "grid", None, None), P("mode", None, "grid", None, None))
    return jax.shard_map(
        per_device,
        mesh=mesh,
        in_specs=placed,
        out_specs=(P("grid", "mode"), P("grid", "mode"), P("grid", "mode")),
        check_vma=False,
    )
```

profile of v0, /device:TPU:0, one launch (start us, length us, event | category | flops | bytes accessed | tf_op | source)
XLA Modules:
  0.0 1810.9 jit_solution(7628288932371613739)
XLA Ops:
  85.5 1080.5 %while.23 = (s32[]{:T(128)}, f32[14,224,4,32]{1,3,2,0:T(8,128)}, f32[14,256,4,32]{1,3,2,0:T(8,128)}, bf16[32,3,2048]{2,0,1:T(8,128)(2,1)S(1)}, bf16[14,4,3,3,204...) while((s32[]{:T(128)}, f32[14,224,4,32]{1,3,2,0:T(8,128)}, ...), condition=%wide.region_4.5_spmd, body=%wide.region_3.4_spmd.sunk | while | flops 794464256 | bytes 77807896 | solution.py:95
  107.4 25.3 %add_convert_fusion.8 = bf16[4,224,3,2048]{1,0,3,2:T(4,128)(2,1)} fusion(f32[4,3,2048]{0,2,1:T(8,128)S(1)} %copy.110, f32[224,2048]{0,1:T(8,128)} %get-tuple-element.268, f32[4,3,2048]{0,2,1:T(8,128)} %copy.111, f32[224,2048]{0,1:T(8,128)} %get-tuple-element.269, f32[4,3,2048]{0,2,1:T(8,128)} %copy.112, f32[224,2048]{0,1:T(8,128)} %get-tuple-element.270), kind=kLoop, calls=%fused_computation.14.clone.1 | loop fusion | flops 33030144 | bytes 16809984 | tf_op jit(solution)/shard_map/while/body/eval_jaxpr/convert_element_type | solution.py:44
  132.7 23.0 %convert_element_type.224 = bf16[896,6144]{0,1:T(8,128)(2,1)} reshape(bf16[4,224,3,2048]{1,0,3,2:T(4,128)(2,1)} %add_convert_fusion.8) | data formatting | bytes 22020096 | tf_op jit(solution)/shard_map/while/body/eval_jaxpr/convert_element_type | solution.py:44
  184.6 25.3 %add_convert_fusion.8 = bf16[4,224,3,2048]{1,0,3,2:T(4,128)(2,1)} fusion(f32[4,3,2048]{0,2,1:T(8,128)S(1)} %copy.110, f32[224,2048]{0,1:T(8,128)} %get-tuple-element.268, f32[4,3,2048]{0,2,1:T(8,128)} %copy.111, f32[224,2048]{0,1:T(8,128)} %get-tuple-element.269, f32[4,3,2048]{0,2,1:T(8,128)} %copy.112, f32[224,2048]{0,1:T(8,128)} %get-tuple-element.270), kind=kLoop, calls=%fused_computation.14.clone.1 | loop fusion | flops 33030144 | bytes 16809984 | tf_op jit(solution)/shard_map/while/body/eval_jaxpr/convert_element_type | solution.py:44
  209.9 23.0 %convert_element_type.224 = bf16[896,6144]{0,1:T(8,128)(2,1)} reshape(bf16[4,224,3,2048]{1,0,3,2:T(4,128)(2,1)} %add_convert_fusion.8) | data formatting | bytes 22020096 | tf_op jit(solution)/shard_map/while/body/eval_jaxpr/convert_element_type | solution.py:44
  261.8 25.3 %add_convert_fusion.8 = bf16[4,224,3,2048]{1,0,3,2:T(4,128)(2,1)} fusion(f32[4,3,2048]{0,2,1:T(8,128)S(1)} %copy.110, f32[224,2048]{0,1:T(8,128)} %get-tuple-element.268, f32[4,3,2048]{0,2,1:T(8,128)} %copy.111, f32[224,2048]{0,1:T(8,128)} %get-tuple-element.269, f32[4,3,2048]{0,2,1:T(8,128)} %copy.112, f32[224,2048]{0,1:T(8,128)} %get-tuple-element.270), kind=kLoop, calls=%fused_computation.14.clone.1 | loop fusion | flops 33030144 | bytes 16809984 | tf_op jit(solution)/shard_map/while/body/eval_jaxpr/convert_element_type | solution.py:44
  287.1 23.0 %convert_element_type.224 = bf16[896,6144]{0,1:T(8,128)(2,1)} reshape(bf16[4,224,3,2048]{1,0,3,2:T(4,128)(2,1)} %add_convert_fusion.8) | data formatting | bytes 22020096 | tf_op jit(solution)/shard_map/while/body/eval_jaxpr/convert_element_type | solution.py:44
  339.0 25.3 %add_convert_fusion.8 = bf16[4,224,3,2048]{1,0,3,2:T(4,128)(2,1)} fusion(f32[4,3,2048]{0,2,1:T(8,128)S(1)} %copy.110, f32[224,2048]{0,1:T(8,128)} %get-tuple-element.268, f32[4,3,2048]{0,2,1:T(8,128)} %copy.111, f32[224,2048]{0,1:T(8,128)} %get-tuple-element.269, f32[4,3,2048]{0,2,1:T(8,128)} %copy.112, f32[224,2048]{0,1:T(8,128)} %get-tuple-element.270), kind=kLoop, calls=%fused_computation.14.clone.1 | loop fusion | flops 33030144 | bytes 16809984 | tf_op jit(solution)/shard_map/while/body/eval_jaxpr/convert_element_type | solution.py:44
  364.3 23.0 %convert_element_type.224 = bf16[896,6144]{0,1:T(8,128)(2,1)} reshape(bf16[4,224,3,2048]{1,0,3,2:T(4,128)(2,1)} %add_convert_fusion.8) | data formatting | bytes 22020096 | tf_op jit(solution)/shard_map/while/body/eval_jaxpr/convert_element_type | solution.py:44
  416.2 25.3 %add_convert_fusion.8 = bf16[4,224,3,2048]{1,0,3,2:T(4,128)(2,1)} fusion(f32[4,3,2048]{0,2,1:T(8,128)S(1)} %copy.110, f32[224,2048]{0,1:T(8,128)} %get-tuple-element.268, f32[4,3,2048]{0,2,1:T(8,128)} %copy.111, f32[224,2048]{0,1:T(8,128)} %get-tuple-element.269, f32[4,3,2048]{0,2,1:T(8,128)} %copy.112, f32[224,2048]{0,1:T(8,128)} %get-tuple-element.270), kind=kLoop, calls=%fused_computation.14.clone.1 | loop fusion | flops 33030144 | bytes 16809984 | tf_op jit(solution)/shard_map/while/body/eval_jaxpr/convert_element_type | solution.py:44
  441.5 23.0 %convert_element_type.224 = bf16[896,6144]{0,1:T(8,128)(2,1)} reshape(bf16[4,224,3,2048]{1,0,3,2:T(4,128)(2,1)} %add_convert_fusion.8) | data formatting | bytes 22020096 | tf_op jit(solution)/shard_map/while/body/eval_jaxpr/convert_element_type | solution.py:44
  493.3 25.3 %add_convert_fusion.8 = bf16[4,224,3,2048]{1,0,3,2:T(4,128)(2,1)} fusion(f32[4,3,2048]{0,2,1:T(8,128)S(1)} %copy.110, f32[224,2048]{0,1:T(8,128)} %get-tuple-element.268, f32[4,3,2048]{0,2,1:T(8,128)} %copy.111, f32[224,2048]{0,1:T(8,128)} %get-tuple-element.269, f32[4,3,2048]{0,2,1:T(8,128)} %copy.112, f32[224,2048]{0,1:T(8,128)} %get-tuple-element.270), kind=kLoop, calls=%fused_computation.14.clone.1 | loop fusion | flops 33030144 | bytes 16809984 | tf_op jit(solution)/shard_map/while/body/eval_jaxpr/convert_element_type | solution.py:44
  518.6 23.0 %convert_element_type.224 = bf16[896,6144]{0,1:T(8,128)(2,1)} reshape(bf16[4,224,3,2048]{1,0,3,2:T(4,128)(2,1)} %add_convert_fusion.8) | data formatting | bytes 22020096 | tf_op jit(solution)/shard_map/while/body/eval_jaxpr/convert_element_type | solution.py:44
  570.5 25.3 %add_convert_fusion.8 = bf16[4,224,3,2048]{1,0,3,2:T(4,128)(2,1)} fusion(f32[4,3,2048]{0,2,1:T(8,128)S(1)} %copy.110, f32[224,2048]{0,1:T(8,128)} %get-tuple-element.268, f32[4,3,2048]{0,2,1:T(8,128)} %copy.111, f32[224,2048]{0,1:T(8,128)} %get-tuple-element.269, f32[4,3,2048]{0,2,1:T(8,128)} %copy.112, f32[224,2048]{0,1:T(8,128)} %get-tuple-element.270), kind=kLoop, calls=%fused_computation.14.clone.1 | loop fusion | flops 33030144 | bytes 16809984 | tf_op jit(solution)/shard_map/while/body/eval_jaxpr/convert_element_type | solution.py:44
  595.8 23.0 %convert_element_type.224 = bf16[896,6144]{0,1:T(8,128)(2,1)} reshape(bf16[4,224,3,2048]{1,0,3,2:T(4,128)(2,1)} %add_convert_fusion.8) | data formatting | bytes 22020096 | tf_op jit(solution)/shard_map/while/body/eval_jaxpr/convert_element_type | solution.py:44
  647.7 25.3 %add_convert_fusion.8 = bf16[4,224,3,2048]{1,0,3,2:T(4,128)(2,1)} fusion(f32[4,3,2048]{0,2,1:T(8,128)S(1)} %copy.110, f32[224,2048]{0,1:T(8,128)} %get-tuple-element.268, f32[4,3,2048]{0,2,1:T(8,128)} %copy.111, f32[224,2048]{0,1:T(8,128)} %get-tuple-element.269, f32[4,3,2048]{0,2,1:T(8,128)} %copy.112, f32[224,2048]{0,1:T(8,128)} %get-tuple-element.270), kind=kLoop, calls=%fused_computation.14.clone.1 | loop fusion | flops 33030144 | bytes 16809984 | tf_op jit(solution)/shard_map/while/body/eval_jaxpr/convert_element_type | solution.py:44
  673.0 23.0 %convert_element_type.224 = bf16[896,6144]{0,1:T(8,128)(2,1)} reshape(bf16[4,224,3,2048]{1,0,3,2:T(4,128)(2,1)} %add_convert_fusion.8) | data formatting | bytes 22020096 | tf_op jit(solution)/shard_map/while/body/eval_jaxpr/convert_element_type | solution.py:44
  724.9 25.3 %add_convert_fusion.8 = bf16[4,224,3,2048]{1,0,3,2:T(4,128)(2,1)} fusion(f32[4,3,2048]{0,2,1:T(8,128)S(1)} %copy.110, f32[224,2048]{0,1:T(8,128)} %get-tuple-element.268, f32[4,3,2048]{0,2,1:T(8,128)} %copy.111, f32[224,2048]{0,1:T(8,128)} %get-tuple-element.269, f32[4,3,2048]{0,2,1:T(8,128)} %copy.112, f32[224,2048]{0,1:T(8,128)} %get-tuple-element.270), kind=kLoop, calls=%fused_computation.14.clone.1 | loop fusion | flops 33030144 | bytes 16809984 | tf_op jit(solution)/shard_map/while/body/eval_jaxpr/convert_element_type | solution.py:44
  802.1 25.3 %add_convert_fusion.8 = bf16[4,224,3,2048]{1,0,3,2:T(4,128)(2,1)} fusion(f32[4,3,2048]{0,2,1:T(8,128)S(1)} %copy.110, f32[224,2048]{0,1:T(8,128)} %get-tuple-element.268, f32[4,3,2048]{0,2,1:T(8,128)} %copy.111, f32[224,2048]{0,1:T(8,128)} %get-tuple-element.269, f32[4,3,2048]{0,2,1:T(8,128)} %copy.112, f32[224,2048]{0,1:T(8,128)} %get-tuple-element.270), kind=kLoop, calls=%fused_computation.14.clone.1 | loop fusion | flops 33030144 | bytes 16809984 | tf_op jit(solution)/shard_map/while/body/eval_jaxpr/convert_element_type | solution.py:44
  879.2 25.3 %add_convert_fusion.8 = bf16[4,224,3,2048]{1,0,3,2:T(4,128)(2,1)} fusion(f32[4,3,2048]{0,2,1:T(8,128)S(1)} %copy.110, f32[224,2048]{0,1:T(8,128)} %get-tuple-element.268, f32[4,3,2048]{0,2,1:T(8,128)} %copy.111, f32[224,2048]{0,1:T(8,128)} %get-tuple-element.269, f32[4,3,2048]{0,2,1:T(8,128)} %copy.112, f32[224,2048]{0,1:T(8,128)} %get-tuple-element.270), kind=kLoop, calls=%fused_computation.14.clone.1 | loop fusion | flops 33030144 | bytes 16809984 | tf_op jit(solution)/shard_map/while/body/eval_jaxpr/convert_element_type | solution.py:44
  904.5 23.0 %convert_element_type.224 = bf16[896,6144]{0,1:T(8,128)(2,1)} reshape(bf16[4,224,3,2048]{1,0,3,2:T(4,128)(2,1)} %add_convert_fusion.8) | data formatting | bytes 22020096 | tf_op jit(solution)/shard_map/while/body/eval_jaxpr/convert_element_type | solution.py:44
  956.4 25.3 %add_convert_fusion.8 = bf16[4,224,3,2048]{1,0,3,2:T(4,128)(2,1)} fusion(f32[4,3,2048]{0,2,1:T(8,128)S(1)} %copy.110, f32[224,2048]{0,1:T(8,128)} %get-tuple-element.268, f32[4,3,2048]{0,2,1:T(8,128)} %copy.111, f32[224,2048]{0,1:T(8,128)} %get-tuple-element.269, f32[4,3,2048]{0,2,1:T(8,128)} %copy.112, f32[224,2048]{0,1:T(8,128)} %get-tuple-element.270), kind=kLoop, calls=%fused_computation.14.clone.1 | loop fusion | flops 33030144 | bytes 16809984 | tf_op jit(solution)/shard_map/while/body/eval_jaxpr/convert_element_type | solution.py:44
  981.7 23.0 %convert_element_type.224 = bf16[896,6144]{0,1:T(8,128)(2,1)} reshape(bf16[4,224,3,2048]{1,0,3,2:T(4,128)(2,1)} %add_convert_fusion.8) | data formatting | bytes 22020096 | tf_op jit(solution)/shard_map/while/body/eval_jaxpr/convert_element_type | solution.py:44
  1033.6 25.3 %add_convert_fusion.8 = bf16[4,224,3,2048]{1,0,3,2:T(4,128)(2,1)} fusion(f32[4,3,2048]{0,2,1:T(8,128)S(1)} %copy.110, f32[224,2048]{0,1:T(8,128)} %get-tuple-element.268, f32[4,3,2048]{0,2,1:T(8,128)} %copy.111, f32[224,2048]{0,1:T(8,128)} %get-tuple-element.269, f32[4,3,2048]{0,2,1:T(8,128)} %copy.112, f32[224,2048]{0,1:T(8,128)} %get-tuple-element.270), kind=kLoop, calls=%fused_computation.14.clone.1 | loop fusion | flops 33030144 | bytes 16809984 | tf_op jit(solution)/shard_map/while/body/eval_jaxpr/convert_element_type | solution.py:44
  1110.8 25.3 %add_convert_fusion.8 = bf16[4,224,3,2048]{1,0,3,2:T(4,128)(2,1)} fusion(f32[4,3,2048]{0,2,1:T(8,128)S(1)} %copy.110, f32[224,2048]{0,1:T(8,128)} %get-tuple-element.268, f32[4,3,2048]{0,2,1:T(8,128)} %copy.111, f32[224,2048]{0,1:T(8,128)} %get-tuple-element.269, f32[4,3,2048]{0,2,1:T(8,128)} %copy.112, f32[224,2048]{0,1:T(8,128)} %get-tuple-element.270), kind=kLoop, calls=%fused_computation.14.clone.1 | loop fusion | flops 33030144 | bytes 16809984 | tf_op jit(solution)/shard_map/while/body/eval_jaxpr/convert_element_type | solution.py:44
  1136.1 23.0 %convert_element_type.224 = bf16[896,6144]{0,1:T(8,128)(2,1)} reshape(bf16[4,224,3,2048]{1,0,3,2:T(4,128)(2,1)} %add_convert_fusion.8) | data formatting | bytes 22020096 | tf_op jit(solution)/shard_map/while/body/eval_jaxpr/convert_element_type | solution.py:44
  1178.1 89.3 %while.22 = (s32[]{:T(128)}, f32[2,256,1024]{1,2,0:T(8,128)}, bf16[256,3,2048]{0,2,1:T(8,128)(2,1)}, bf16[2,4,3,3,2048]{4,1,3,2,0:T(4,128)(2,1)S(1)}, bf16[256,6144]{1,0:T(8,128)(2,1)}, /*index=5*/s32[]{:T(128)}) while((s32[]{:T(128)}, f32[2,256,1024]{1,2,0:T(8,128)}, bf16[256,3,2048]{0,2,1:T(8,128)(2,1)}, ...), condition=%wide.region_1.2_spmd, body=%wide.region_0.1_spmd.sunk | while | flops 3260882944 | bytes 91013328 | solution.py:81
  1189.4 24.4 %add_convert_fusion.6 = bf16[4,256,3,2048]{1,0,3,2:T(4,128)(2,1)S(1)} fusion(f32[4,3,2048]{0,2,1:T(8,128)S(1)} %copy.100, f32[256,2048]{0,1:T(8,128)} %get-tuple-element.249, f32[4,3,2048]{0,2,1:T(8,128)} %copy.101, f32[256,2048]{0,1:T(8,128)} %get-tuple-element.251, f32[4,3,2048]{0,2,1:T(8,128)} %copy.102, f32[256,2048]{0,1:T(8,128)} %get-tuple-element.253), kind=kLoop, calls=%fused_computation.clone.1 | loop fusion | flops 37748736 | bytes 19169280 | tf_op jit(solution)/shard_map/while/body/eval_jaxpr/convert_element_type | solution.py:44
  1233.9 24.4 %add_convert_fusion.6 = bf16[4,256,3,2048]{1,0,3,2:T(4,128)(2,1)S(1)} fusion(f32[4,3,2048]{0,2,1:T(8,128)S(1)} %copy.100, f32[256,2048]{0,1:T(8,128)} %get-tuple-element.249, f32[4,3,2048]{0,2,1:T(8,128)} %copy.101, f32[256,2048]{0,1:T(8,128)} %get-tuple-element.251, f32[4,3,2048]{0,2,1:T(8,128)} %copy.102, f32[256,2048]{0,1:T(8,128)} %get-tuple-element.253), kind=kLoop, calls=%fused_computation.clone.1 | loop fusion | flops 37748736 | bytes 19169280 | tf_op jit(solution)/shard_map/while/body/eval_jaxpr/convert_element_type | solution.py:44
  1272.3 203.4 %all-reduce.3.cloned.1.call-done = f32[224,1792]{0,1:T(8,128)} async-done(((f32[224,1792]{0,1:T(8,128)}), f32[224,1792]{0,1:T(8,128)}) %all-reduce.3.cloned.1.call-update) | async-done | bytes 1605648
  1478.4 163.8 %reduce-scatter.8.cloned.1.call-done = f32[8,1792]{1,0:T(8,128)} async-done(((f32[256,1792]{1,0:T(8,128)}), f32[8,1792]{1,0:T(8,128)}) %reduce-scatter.8.cloned.1.call-update) | async-done | bytes 57360
  1642.2 162.1 %reduce-scatter.6.cloned.1.call-done = f32[8,2048]{1,0:T(8,128)} async-done(((f32[256,2048]{1,0:T(8,128)}), f32[8,2048]{1,0:T(8,128)}) %reduce-scatter.6.cloned.1.call-update) | async-done | bytes 65552 | tf_op jit(solution)/shard_map/reduce_scatter | solution.py:99
  (557 shorter events, 608.2 us)
Async XLA Ops:
  7.2 56.1 %all-gather.2.cloned.1.call-start = ((), (), s32[]{:S(2)}) async-start(), calls=%async_computation.2 | async-start | bytes 3440640 | tf_op jit(solution)/shard_map/all_gather | solution.py:62
  7.9 1467.8 %all-reduce.3.cloned.1.call-start = ((), (), s32[]{:S(2)}) async-start(), calls=%async_computation.5 | async-start | bytes 3670016
  10.3 38.4 %collective-permute-start.1 = (bf16[64,3,1,4,128]{4,3,2,1,0:T(4,128)(2,1)}, bf16[64,3,1,4,128]{4,3,2,1,0:T(4,128)(2,1)}, u32[]{:S(2)}, u32[]{:S(2)}) collective-permute-start(bf16[64,3,1,4,128]{4,3,2,1,0:T(4,128)(2,1)} %get-tuple-element.156), channel_id=1, source_target_pairs={{4,0},{8,4},{12,8},{16,12},{20,16},{24,20},{28,24},{32,28},{36,32}... | collective-permute-start | bytes 589832 | tf_op jit(solution)/shard_map/ppermute | solution.py:18
  16.9 31.8 %collective-permute-start = (bf16[64,3,1,4,128]{4,3,2,1,0:T(4,128)(2,1)}, bf16[64,3,1,4,128]{4,3,2,1,0:T(4,128)(2,1)}, u32[]{:S(2)}, u32[]{:S(2)}) collective-permute-start(bf16[64,3,1,4,128]{4,3,2,1,0:T(4,128)(2,1)} %get-tuple-element.155), channel_id=1, source_target_pairs={{0,4},{4,8},{8,12},{12,16},{16,20},{20,24},{24,28},{28,32},{32,36}... | collective-permute-start | bytes 589832 | tf_op jit(solution)/shard_map/ppermute | solution.py:16
  71.9 10.0 copy-start
  155.8 6.1 copy-start.10
  155.8 6.9 copy-start.6
  232.9 6.1 copy-start.10
  232.9 6.9 copy-start.6
  310.1 6.1 copy-start.10
  310.1 6.9 copy-start.6
  387.3 6.9 copy-start.6
  464.5 6.1 copy-start.10
  464.5 6.9 copy-start.6
  541.7 6.1 copy-start.10
  541.7 6.9 copy-start.6
  618.8 6.1 copy-start.10
  618.8 6.9 copy-start.6
  696.0 6.9 copy-start.6
  773.2 6.1 copy-start.10
  773.2 6.9 copy-start.6
  850.4 6.1 copy-start.10
  850.4 6.9 copy-start.6
  927.6 6.1 copy-start.10
  927.6 6.9 copy-start.6
  1004.8 6.9 copy-start.6
  1081.9 6.9 copy-start.6
  1159.1 6.9 copy-start.6
  1166.0 476.2 %reduce-scatter.8.cloned.1.call-start = ((), (), s32[]{:S(2)}) async-start(), calls=%async_computation.4 | async-start | bytes 1892352
  1178.0 626.3 %reduce-scatter.6.cloned.1.call-start = ((), (), s32[]{:S(2)}) async-start(), calls=%async_computation.3 | async-start | bytes 2162688 | tf_op jit(solution)/shard_map/reduce_scatter | solution.py:99
  1216.2 6.7 copy-start.14
  1260.7 6.8 copy-start.14
  (76 other events, 146.2 us)
Sparse Core Ops, SparseCore 0:
  9.7 34.4 all-gather.1
  1166.2 309.4 all-reduce.2
  1478.8 163.4 reduce-scatter.7
  1645.0 159.2 reduce-scatter.5
where the time goes:
time: 1820 us; the launch traced here: 1810 us
  local copies, waits for them, and re-layouts  590 us (32%)
  waiting for transfers between devices  530 us (29%)
  other arithmetic  516 us (28%)
  matrix products  137 us (8%)
    convert_element_type x30, other arithmetic, advect(): return (first + second + third).astype(jnp.bfloat16)  426 us
    unnamed x6, waiting for transfers between devices  368 us
    convert_element_type x14, local copies, waits for them, and re-layouts, advect(): return (first + second + third).astype(jnp.bfloat16)  322 us
    reduce_scatter x1, waiting for transfers between devices, per_device(): lax.psum_scatter(new_terms, 'grid', scatter_dimension=0, tiled=True)  162 us
    dot_general x30, matrix products, contract(): lax.dot_general(left, right, (((1,), (1,)), ((), ())), preferred_element_...  137 us
    convert_element_type x30, other arithmetic, advect(): velocity[None, :, None, 0].astype(jnp.float32)  74.8 us
    convert_element_type x30, local copies, waits for them, and re-layouts, advect(): grad_block[:, None, :, 0].astype(jnp.float32)  47 us
    convert_element_type x30, local copies, waits for them, and re-layouts, advect(): grad_block[:, None, :, 1].astype(jnp.float32)  46.7 us
  transfers between devices with their start and end apart: 6, of which 3 were waited for; matrix products, arithmetic and copies ran while one was open for 8% of the time, Pallas kernels for 0%

commit v1 on v0

v1 whole, which is shorter than its diff:
```python
import math

import jax
import jax.numpy as jnp
from jax import lax
from jax.experimental import pallas as pl
from jax.experimental.pallas import tpu as pltpu
from jax.sharding import PartitionSpec as P

MESH = pl.DeviceIdType.MESH
F32 = jnp.float32
BF16 = jnp.bfloat16
PLANES = 4
LINES = 4
LANES = 128
DEPTH = 3 * LINES * LANES
ROWS = 64
HELD = 56
NEW = 8
TOTAL = 256
NEWS = 32
GROUP = 28
HCOLS = GROUP * NEWS
ACOLS = 1024
WEIGHT = 1.0 / 256.0


def row_every(g):
    i = 8 * g
    return 64 * (i // 56) + i % 56 if i < 224 else 64 * ((i - 224) // 8) + 56


def row_held(g):
    i = 7 * g
    return 64 * (i // 56) + i % 56


def kernel(
    own, out_a, out_w, out_q,
    halo, vall, vnew, slope, left, right, acc_h, acc_a,
    f_h, s1_h, r1_h, t1_h, s2_h, r2_h, t2_h, r3_h,
    f_a, s1_a, r1_a, t1_a, s2_a, r2_a, t2_a, r3_a,
    halo_send, halo_recv, gat_send, gat_recv, own_sem,
    rs1_send, rs1_recv, rs2_send, rs2_recv, rs3_send, rs3_recv,
):
    g = lax.axis_index("grid")
    m = lax.axis_index("mode")
    py, px, pz = g // 8, (g // 2) % 4, g % 2
    core = m + 1 - 2 * (m % 2)
    far = (m + 2) % 4
    far_core = (core + 2) % 4

    def cell(y, x, z):
        return (y * 4 + x) * 2 + z

    ahead, behind = (g + 1) % 32, (g + 31) % 32
    along_x = [(cell(py, (px + d) % 4, pz), m) for d in (1, 2, 3)]
    along_y = [(cell((py + d) % 4, px, pz), m) for d in (1, 2, 3)]
    across = (cell(py, px, 1 - pz), m)

    barrier = pltpu.get_barrier_semaphore()
    greeted = [(ahead, m), (behind, m), (g, core), (g, far), across] + along_x + along_y
    for other in greeted:
        pl.semaphore_signal(barrier, inc=1, device_id=other, device_id_type=MESH)
    pl.semaphore_wait(barrier, len(greeted))

    def remote(src, dst, send, recv, device):
        return pltpu.make_async_remote_copy(
            src_ref=src, dst_ref=dst, send_sem=send, recv_sem=recv,
            device_id=device, device_id_type=MESH,
        )

    def slot(who):
        return pl.ds(pl.multiple_of(who * ROWS, ROWS), ROWS)

    to_ahead = remote(own.at[PLANES - 1], halo.at[0], halo_send.at[0], halo_recv.at[0], (ahead, m))
    to_behind = remote(own.at[0], halo.at[1], halo_send.at[1], halo_recv.at[1], (behind, m))

    def to_far(x):
        return remote(own.at[x], vall.at[x, slot(m)], gat_send.at[0, x], gat_recv.at[0, x], (g, far))

    def to_core(x):
        return remote(own.at[x], vall.at[x, slot(m)], gat_send.at[1, x], gat_recv.at[1, x], (g, core))

    def pass_on(x):
        return remote(
            vall.at[x, slot(far)], vall.at[x, slot(far)], gat_send.at[2, x], gat_recv.at[2, x], (g, core)
        )

    def keep(x):
        return pltpu.make_async_copy(own.at[x], vall.at[x, slot(m)], own_sem.at[x])

    to_ahead.start()
    to_behind.start()
    for x in range(PLANES):
        to_far(x).start()
        to_core(x).start()
        keep(x).start()

    def part(ref, index, a, y):
        return ref[index, :, (a * LINES + y) * LANES : (a * LINES + y + 1) * LANES].astype(F32)

    to_ahead.wait()
    to_behind.wait()
    for x in range(PLANES):
        for a in range(3):
            centre = [part(own, x, a, y) for y in range(LINES)]
            for y in range(LINES):
                after = part(own, x + 1, a, y) if x + 1 < PLANES else part(halo, 1, a, y)
                before = part(own, x - 1, a, y) if x > 0 else part(halo, 0, a, y)
                slope[x, a, y] = (after - before) * 0.5
                slope[x, 3 + a, y] = (centre[(y + 1) % LINES] - centre[(y - 1) % LINES]) * 0.5
                slope[x, 6 + a, y] = (
                    pltpu.roll(centre[y], LANES - 1, 1) - pltpu.roll(centre[y], 1, 1)
                ) * 0.5

    def spread(x, a, b, y, k):
        row = slope[x, b * 3 + a, y, k : k + 1, :]
        return jnp.broadcast_to(row, (16, LANES)).astype(BF16)[None]

    def lanes(a, y):
        return slice((a * LINES + y) * LANES, (a * LINES + y + 1) * LANES)

    def build_held(x, half, into):
        for y in range(LINES):
            v = [vnew[x, :, lanes(b, y)].reshape(2, 16, LANES) for b in range(3)]
            for k in range(GROUP):
                s = [[spread(x, a, b, y, half * GROUP + k) for b in range(3)] for a in range(3)]
                for c in range(3):
                    w = v[0] * s[0][c] + v[1] * s[1][c] + v[2] * s[2][c]
                    into[k * NEWS : (k + 1) * NEWS, lanes(c, y)] = w.reshape(NEWS, LANES)
                for c in range(3):
                    q = v[0] * s[c][0] + v[1] * s[c][1] + v[2] * s[c][2]
                    into[HCOLS + k * NEWS : HCOLS + (k + 1) * NEWS, lanes(c, y)] = q.reshape(NEWS, LANES)

    def build_new(x, half, into):
        for y in range(LINES):
            for k in range(4):
                s = [[spread(x, a, b, y, HELD + half * 4 + k) for b in range(3)] for a in range(3)]
                v = [vall[x, :, lanes(b, y)].reshape(16, 16, LANES) for b in range(3)]
                for c in range(3):
                    q = v[0] * s[c][0] + v[1] * s[c][1] + v[2] * s[c][2]
                    into[k * TOTAL : (k + 1) * TOTAL, lanes(c, y)] = q.reshape(TOTAL, LANES)

    def contract(x, block):
        return lax.dot_general(
            vall[x], block, (((1,), (1,)), ((), ())), preferred_element_type=F32
        )

    def arrive(x):
        to_far(x).wait_recv()
        pass_on(x).start()
        keep(x).wait()
        to_core(x).wait_recv()
        pass_on(x).wait_recv()
        for pair in range(2):
            tops = [
                vall[x, (2 * pair + e) * ROWS + 48 : (2 * pair + e) * ROWS + 64, :].astype(F32)[8:16]
                for e in range(2)
            ]
            vnew[x, pair * 16 : (pair + 1) * 16, :] = jnp.concatenate(tops, 0).astype(BF16)

    acc_h[...] = jnp.zeros_like(acc_h)
    acc_a[...] = jnp.zeros_like(acc_a)
    arrive(0)
    build_held(0, 0, left)

    def plane(x, carry):
        build_held(x, 1, right)
        acc_h[0] += contract(x, left[...])

        @pl.when(x < PLANES - 1)
        def _():
            arrive(x + 1)

        build_held(jnp.minimum(x + 1, PLANES - 1), 0, left)
        acc_h[1] += contract(x, right[...])
        return carry

    lax.fori_loop(0, PLANES, plane, 0)

    class Job:
        def __init__(self, n, bufs, width, source, maps, sinks):
            self.n, self.width, self.source, self.maps, self.sinks = n, width, source, maps, sinks
            self.f, self.s1, self.r1, self.t1, self.s2, self.r2, self.t2, self.r3 = bufs

        def first(self):
            for e in range(2):
                for p in range(4):
                    for q in range(4):
                        at = (q * 4 + p) if e == 0 else (p * 4 + q)
                        rows = [self.maps[e](2 * at + z) for z in range(2)]
                        for z in range(2):
                            self.f[e, p, q * 16 + z * 8 : q * 16 + z * 8 + 8, :] = self.source(e, rows[z])
                        self.s1[e, p, q * 16 : q * 16 + 16, :] = self.f[e, p, q * 16 : q * 16 + 16, :].astype(BF16)
            for copy in self.copies1():
                copy.start()

        def copies1(self):
            found = []
            for d in (1, 2, 3):
                for e in range(2):
                    p = ((px if e == 0 else py) + d) % 4
                    found.append(
                        remote(
                            self.s1.at[e, p], self.r1.at[e, d - 1],
                            rs1_send.at[self.n, e, d - 1], rs1_recv.at[self.n, e, d - 1],
                            (along_x if e == 0 else along_y)[d - 1],
                        )
                    )
            return found

        def second(self):
            for copy in self.copies1():
                copy.wait()
            for e in range(2):
                p = px if e == 0 else py
                t = self.f[e, p]
                for d in range(3):
                    t = t + self.r1[e, d].astype(F32)
                for q in range(4):
                    self.t1[e, q] = t[q * 16 : q * 16 + 16]
                    self.s2[e, q] = t[q * 16 : q * 16 + 16].astype(BF16)
            for copy in self.copies2():
                copy.start()

        def copies2(self):
            found = []
            for d in (1, 2, 3):
                for e in range(2):
                    q = ((py if e == 0 else px) + d) % 4
                    found.append(
                        remote(
                            self.s2.at[e, q], self.r2.at[e, d - 1],
                            rs2_send.at[self.n, e, d - 1], rs2_recv.at[self.n, e, d - 1],
                            (along_y if e == 0 else along_x)[d - 1],
                        )
                    )
            return found

        def third(self):
            for copy in self.copies2():
                copy.wait()
            for e in range(2):
                t = self.t1[e, py if e == 0 else px]
                for d in range(3):
                    t = t + self.r2[e, d].astype(F32)
                self.t2[e, 0] = t[0:8]
                self.t2[e, 1] = t[8:16]
            for copy in self.copies3():
                copy.start()

        def copies3(self):
            return [
                remote(
                    self.t2.at[e, 1 - pz], self.r3.at[e],
                    rs3_send.at[self.n, e], rs3_recv.at[self.n, e], across,
                )
                for e in range(2)
            ]

        def last(self):
            for copy in self.copies3():
                copy.wait()
            for e in range(2):
                ref, at = self.sinks[e]
                ref[:, at : at + self.width] = (self.t2[e, pz] + self.r3[e]) * WEIGHT

    def held_job(half):
        def source(e, row):
            return acc_h[half, row : row + 8, e * HCOLS : (e + 1) * HCOLS]

        bufs = [b.at[half] for b in (f_h, s1_h, r1_h, t1_h, s2_h, r2_h, t2_h, r3_h)]
        return Job(half, bufs, HCOLS, source, (row_every, row_held),
                   ((out_w, half * HCOLS), (out_q, half * HCOLS)))

    def new_job():
        def source(e, row):
            return acc_a[e, row : row + 8, :]

        return Job(2, (f_a, s1_a, r1_a, t1_a, s2_a, r2_a, t2_a, r3_a), ACOLS, source,
                   (row_every, row_every), ((out_a, 0), (out_a, ACOLS)))

    jobs = [held_job(0), held_job(1), new_job()]
    jobs[0].first()
    jobs[1].first()

    build_new(0, 0, left.at[0:ACOLS])

    def new_plane(x):
        build_new(x, 1, right.at[0:ACOLS])
        acc_a[0] += contract(x, left[0:ACOLS])
        if x + 1 < PLANES:
            build_new(x + 1, 0, left.at[0:ACOLS])
        acc_a[1] += contract(x, right[0:ACOLS])

    new_plane(0)
    new_plane(1)
    jobs[0].second()
    new_plane(2)
    jobs[1].second()
    new_plane(3)
    jobs[2].first()
    jobs[0].third()
    jobs[1].third()
    jobs[0].last()
    jobs[1].last()
    jobs[2].second()
    jobs[2].third()
    jobs[2].last()
    for x in range(PLANES):
        to_far(x).wait_send()
        to_core(x).wait_send()
        pass_on(x).wait_send()


def rs_scratch(lead, width):
    return [
        pltpu.VMEM(lead + (2, 4, 64, width), F32),
        pltpu.VMEM(lead + (2, 4, 64, width), BF16),
        pltpu.VMEM(lead + (2, 3, 64, width), BF16),
        pltpu.VMEM(lead + (2, 4, 16, width), F32),
        pltpu.VMEM(lead + (2, 4, 16, width), BF16),
        pltpu.VMEM(lead + (2, 3, 16, width), BF16),
        pltpu.VMEM(lead + (2, 2, 8, width), F32),
        pltpu.VMEM(lead + (2, 8, width), F32),
    ]


def per_device(held_modes, new_modes):
    own = jnp.concatenate(
        [
            held_modes.transpose(2, 0, 1, 3, 4).reshape(PLANES, HELD, DEPTH),
            new_modes.transpose(2, 0, 1, 3, 4).reshape(PLANES, NEW, DEPTH),
        ],
        1,
    )
    vmem = pl.BlockSpec(memory_space=pltpu.VMEM)
    dma = pltpu.SemaphoreType.DMA
    out_a, out_w, out_q = pl.pallas_call(
        kernel,
        out_shape=(
            jax.ShapeDtypeStruct((8, 2 * ACOLS), F32),
            jax.ShapeDtypeStruct((8, 2 * HCOLS), F32),
            jax.ShapeDtypeStruct((8, 2 * HCOLS), F32),
        ),
        in_specs=[vmem],
        out_specs=(vmem, vmem, vmem),
        scratch_shapes=[
            pltpu.VMEM((2, ROWS, DEPTH), BF16),
            pltpu.VMEM((PLANES, TOTAL, DEPTH), BF16),
            pltpu.VMEM((PLANES, NEWS, DEPTH), BF16),
            pltpu.VMEM((PLANES, 9, LINES, ROWS, LANES), F32),
            pltpu.VMEM((2 * HCOLS, DEPTH), BF16),
            pltpu.VMEM((2 * HCOLS, DEPTH), BF16),
            pltpu.VMEM((2, TOTAL, 2 * HCOLS), F32),
            pltpu.VMEM((2, TOTAL, ACOLS), F32),
            *rs_scratch((2,), HCOLS),
            *rs_scratch((), ACOLS),
            dma((2,)),
            dma((2,)),
            dma((3, PLANES)),
            dma((3, PLANES)),
            dma((PLANES,)),
            dma((3, 2, 3)),
            dma((3, 2, 3)),
            dma((3, 2, 3)),
            dma((3, 2, 3)),
            dma((3, 2)),
            dma((3, 2)),
        ],
        compiler_params=pltpu.CompilerParams(
            collective_id=0, has_side_effects=True, vmem_limit_bytes=60 * 2**20
        ),
        cost_estimate=pl.CostEstimate(
            flops=2 * 5632 * TOTAL * PLANES * DEPTH, bytes_accessed=2**20, transcendentals=0
        ),
    )(own)
    by_mode = out_a.reshape(8, NEW, 4, ROWS)
    new_third = jnp.concatenate(
        [by_mode[..., :HELD].reshape(8, NEW, 4 * HELD), by_mode[..., HELD:].reshape(8, NEW, NEWS)], 2
    ).reshape(8, 2 * ACOLS)
    return (new_third, out_w, out_q[:7])


def solution(mesh):
    placed = (P("mode", None, "grid", None, None), P("mode", None, "grid", None, None))
    return jax.shard_map(
        per_device,
        mesh=mesh,
        in_specs=placed,
        out_specs=(P("grid", "mode"), P("grid", "mode"), P("grid", "mode")),
        check_vma=False,
    )
```

time: 1820 us -> 95.6 us (0.05)
  local copies, waits for them, and re-layouts: 590 us -> 5.15 us
  waiting for transfers between devices: 530 us -> 0 us
  other arithmetic: 516 us -> 1.67 us
  matrix products: 137 us -> 0 us
  Pallas kernels: 0 us -> 87.8 us
    convert_element_type x78 -> x0, other arithmetic: 504 us -> none  [the longest x30 426 us: advect(): return (first + second + third).astype(jnp.bfloat16)]
    convert_element_type x104 -> x0, local copies, waits for them, and re-layouts: 445 us -> none  [the longest x14 322 us: advect(): return (first + second + third).astype(jnp.bfloat16)]
    unnamed x6 -> x0, waiting for transfers between devices: 368 us -> none
    reduce_scatter x1 -> x0, waiting for transfers between devices: 162 us -> none  [per_device(): lax.psum_scatter(new_terms, 'grid', scatter_dimension=0, tiled=True)]
    dot_general x30 -> x0, matrix products: 137 us -> none  [contract(): lax.dot_general(left, right, (((1,), (1,)), ((), ())), preferred_element_...]
    pallas_call x0 -> x1, Pallas kernels: none -> 87.8 us  [per_device(): pl.pallas_call(kernel, out_shape=(jax.ShapeDtypeStruct((8, 2 * ACOLS), F3...]
    while x204 -> x0, local copies, waits for them, and re-layouts: 47 us -> none
    dynamic_update_slice x28 -> x0, local copies, waits for them, and re-layouts: 19 us -> none  [per_device(): lax.scan(held_step, jnp.zeros((), jnp.float32), held_slopes)]
  transfers between devices with their start and end apart: 6 -> 0, of which waited for: 3 -> 0; matrix products, arithmetic and copies ran while one was open for 8% -> 0% of each run, Pallas kernels for 0% -> 0%
where the time goes in v1:
time: 95.6 us; the launch traced here: 95.3 us
  Pallas kernels  87.8 us (92%)
  local copies, waits for them, and re-layouts  5.15 us (5%)
  other arithmetic  1.67 us (2%)
    pallas_call x1, Pallas kernels, per_device(): pl.pallas_call(kernel, out_shape=(jax.ShapeDtypeStruct((8, 2 * ACOLS), F3...  87.8 us

profile of v1, /device:TPU:0, one launch (start us, length us, event | category | flops | bytes accessed | tf_op | source)
XLA Modules:
  0.0 95.3 jit_solution(4248590411944230309)
XLA Ops:
  0.6 0.9 copy.6
  1.6 1.3 %copy.5 = bf16[4,56,3,4,128]{4,3,2,1,0:T(4,128)(2,1)S(1)} copy(bf16[4,56,3,4,128]{4,3,0,2,1:T(4,128)(2,1)} %bitcast.7) | data formatting | bytes 1376256 | tf_op jit(solution)/shard_map/transpose | solution.py:333
  2.9 0.3 reshape.24
  3.2 1.0 %pad_maximum_fusion.own = bf16[4,64,1536]{2,1,0:T(8,128)(2,1)} fusion(bf16[4,8,1536]{2,1,0:T(8,128)(2,1)S(1)} %bitcast.8, bf16[4,56,1536]{2,1,0:T(8,128)(2,1)S(1)} %reshape.24), kind=kLoop, calls=%fused_computation | loop fusion | flops 1572864 | bytes 1572864 | tf_op jit(solution)/shard_map/concatenate | solution.py:331
  4.1 87.8 %shard_map.49 = (f32[8,2048]{1,0:T(8,128)}, f32[8,1792]{1,0:T(8,128)}, f32[8,1792]{1,0:T(8,128)}) custom-call(bf16[4,64,1536]{2,1,0:T(8,128)(2,1)} %pad_maximum_fusion.own), custom_call_target="tpu_custom_call" | custom-call | flops 17716740096 | bytes 1048576 | tf_op jit(solution)/shard_map/pallas_call | solution.py:340
  91.9 0.0 copy-start.1
  91.9 0.0 copy-start
  92.0 1.0 %reshape.26 = f32[8,8,4,64]{3,2,1,0:T(4,128)S(1)} reshape(f32[8,2048]{1,0:T(8,128)} %get-tuple-element.6) | data formatting | bytes 131072 | tf_op jit(solution)/shard_map/reshape | solution.py:379
  92.9 0.1 reshape.27
  93.1 0.1 slice.13
  93.2 0.1 reshape.28
  93.4 0.7 pad_maximum_fusion.1
  94.1 0.0 copy-done.1
  94.1 0.6 copy.11
  94.7 0.0 copy-done
  94.7 0.6 copy.12
  (2 shorter events, 0.0 us)
Async XLA Ops:
  91.9 2.1 %copy-start.1 = (f32[8,1792]{1,0:T(8,128)S(1)}, f32[8,1792]{1,0:T(8,128)}, u32[]{:S(2)}) copy-start(f32[8,1792]{1,0:T(8,128)} %get-tuple-element.13) | copy-start | bytes 172036
  91.9 2.8 %copy-start = (f32[8,1792]{1,0:T(8,128)S(1)}, f32[8,1792]{1,0:T(8,128)}, u32[]{:S(2)}) copy-start(f32[8,1792]{1,0:T(8,128)} %get-tuple-element.8) | copy-start | bytes 172036

commit v2 on v1

v2 whole, which is shorter than its diff:
```python
import jax
import jax.numpy as jnp
from jax import lax
from jax.experimental import pallas as pl
from jax.experimental.pallas import tpu as pltpu
from jax.sharding import PartitionSpec as P

MESH = pl.DeviceIdType.MESH
F32 = jnp.float32
BF16 = jnp.bfloat16
CHUNKS = 8
ORDER = ((1, 0), (1, 1), (2, 0), (0, 0), (3, 0), (2, 1), (0, 1), (3, 1))
SENDS = (0, 1, 3, 2, 4, 6, 7, 5)
RELAYED = (3, 4, 6, 7)
LANES = 128
PARTS = 6
DEPTH = PARTS * LANES
ROWS = 64
HELD = 56
NEW = 8
TOTAL = 256
NEWS = 32
GROUP = 28
HCOLS = GROUP * NEWS
NTILE = 64
NGROUP = 4
ACOLS = NGROUP * TOTAL
WEIGHT = 1.0 / 256.0


def row_every(g):
    i = 8 * g
    return 64 * (i // 56) + i % 56 if i < 224 else 64 * ((i - 224) // 8) + 56


def row_held(g):
    i = 7 * g
    return 64 * (i // 56) + i % 56


def kernel(
    given, out_a, out_w, out_q,
    own, relay, vall, vnew, slope, left, right, acc_h, acc_a,
    f_h, s1_h, r1_h, t1_h, s2_h, r2_h, t2_h, r3_h,
    f_a, s1_a, r1_a, t1_a, s2_a, r2_a, t2_a, r3_a,
    near_send, near_recv, far_send, far_recv, core_send, core_recv, pass_send, pass_recv,
    halo_send, halo_recv, own_sem, load_sem,
    rs1_send, rs1_recv, rs2_send, rs2_recv, rs3_send, rs3_recv,
):
    g = lax.axis_index("grid")
    m = lax.axis_index("mode")
    py, px, pz = g // 8, (g // 2) % 4, g % 2
    core = m + 1 - 2 * (m % 2)
    far = (m + 2) % 4

    def cell(y, x, z):
        return (y * 4 + x) * 2 + z

    along_x = [(cell(py, (px + d) % 4, pz), m) for d in (1, 2, 3)]
    along_y = [(cell((py + d) % 4, px, pz), m) for d in (1, 2, 3)]
    across = (cell(py, px, 1 - pz), m)
    beyond = (cell(py, px, 1 - pz), far)
    halo_to = ((g + 32 + 2 - 4 * pz) % 32, m)
    halo_from = ((g + 32 - 2 + 4 * pz) % 32, m)

    def load(t):
        x, h = ORDER[t]
        return pltpu.make_async_copy(given.at[x * 2 + h], own.at[t], load_sem.at[t])

    for t in range(CHUNKS):
        load(t).start()
    barrier = pltpu.get_barrier_semaphore()
    greeted = [(g, core), (g, far), across, beyond, halo_to, halo_from] + along_x + along_y
    for other in greeted:
        pl.semaphore_signal(barrier, inc=1, device_id=other, device_id_type=MESH)
    pl.semaphore_wait(barrier, len(greeted))

    def remote(src, dst, send, recv, device):
        return pltpu.make_async_remote_copy(
            src_ref=src, dst_ref=dst, send_sem=send, recv_sem=recv,
            device_id=device, device_id_type=MESH,
        )

    def slot(who):
        return pl.ds(pl.multiple_of(who * ROWS, ROWS), ROWS)

    def leave(t):
        if t in RELAYED:
            r = RELAYED.index(t)
            return remote(own.at[t], relay.at[r], near_send.at[t], near_recv.at[t], across)
        return remote(own.at[t], vall.at[t, :, slot(m)], near_send.at[t], near_recv.at[t], (g, far))

    def onward(t):
        r = RELAYED.index(t)
        return remote(relay.at[r], vall.at[t, :, slot(m)], far_send.at[t], far_recv.at[t], beyond)

    def to_core(t):
        return remote(own.at[t], vall.at[t, :, slot(m)], core_send.at[t], core_recv.at[t], (g, core))

    def pass_on(t):
        return remote(
            vall.at[t, :, slot(far)], vall.at[t, :, slot(far)], pass_send.at[t], pass_recv.at[t], (g, core)
        )

    def keep(t):
        return pltpu.make_async_copy(own.at[t], vall.at[t, :, slot(m)], own_sem.at[t])

    def halo(h):
        return remote(relay.at[2 * h + 1 - pz], relay.at[4 + h], halo_send.at[h], halo_recv.at[h], halo_to)

    load(SENDS[0]).wait()
    leave(SENDS[0]).start()
    for t in SENDS[1:]:
        load(t).wait()
    for t in range(CHUNKS):
        to_core(t).start()
        keep(t).start()

    def slopes(t, other, before, at_before, after, at_after):
        for a in range(3):
            here = [own[t, e * 3 + a].astype(F32) for e in range(2)]
            there = [own[other, e * 3 + a].astype(F32) for e in range(2)]
            for e in range(2):
                up = after[at_after, e * 3 + a].astype(F32)
                down = before[at_before, e * 3 + a].astype(F32)
                slope[t, a, e] = (up - down) * 0.5
                up, down = (here[1], there[1]) if e == 0 else (there[0], here[0])
                slope[t, 3 + a, e] = (up - down) * 0.5
                slope[t, 6 + a, e] = (
                    pltpu.roll(here[e], LANES - 1, 1) - pltpu.roll(here[e], 1, 1)
                ) * 0.5

    def at(x, h):
        return ORDER.index((x, h))

    def slopes_inner(x, h):
        slopes(at(x, h), at(x, 1 - h), own, at(x - 1, h), own, at(x + 1, h))

    def slopes_outer(h):
        slopes(at(0, h), at(0, 1 - h), relay, (4 + h) * (1 - pz) + (2 * h + 1) * pz, own, at(1, h))
        slopes(at(3, h), at(3, 1 - h), own, at(2, h), relay, 2 * h * (1 - pz) + (4 + h) * pz)

    def depart(s):
        if s + 2 < CHUNKS:
            leave(SENDS[s + 2]).start()

    def landed(t):
        leave(t).wait_recv()
        leave(t).wait_send()
        if t in RELAYED:
            onward(t).start()
        else:
            pass_on(t).start()
        depart(SENDS.index(t))

    def shared(t):
        onward(t).wait_recv()
        pass_on(t).start()

    def whole(t):
        keep(t).wait()
        to_core(t).wait_recv()
        pass_on(t).wait_recv()
        for j in range(PARTS):
            tops = [vall[t, j, q * ROWS + 48 : (q + 1) * ROWS, :].astype(F32)[8:16] for q in range(4)]
            vnew[t, j] = jnp.concatenate(tops, 0).astype(BF16)

    def spread(t, a, b, e, k):
        row = slope[t, b * 3 + a, e, k : k + 1, :]
        return jnp.broadcast_to(row, (16, LANES)).astype(BF16)[None]

    def lanes(a, e):
        return slice((e * 3 + a) * LANES, (e * 3 + a + 1) * LANES)

    def contract(t, block):
        return lax.dot_general(
            jnp.concatenate([vall[t, j] for j in range(PARTS)], 1), block,
            (((1,), (1,)), ((), ())), preferred_element_type=F32,
        )

    def build_held(t, half, into):
        base = half * 2 * HCOLS
        for e in range(2):
            v = [vnew[t, e * 3 + b].reshape(2, 16, LANES) for b in range(3)]
            for k in range(GROUP):
                s = [[spread(t, a, b, e, half * GROUP + k) for b in range(3)] for a in range(3)]
                at = base + k * NEWS
                for c in range(3):
                    w = v[0] * s[0][c] + v[1] * s[1][c] + v[2] * s[2][c]
                    into[at : at + NEWS, lanes(c, e)] = w.reshape(NEWS, LANES)
                at = at + HCOLS
                for c in range(3):
                    q = v[0] * s[c][0] + v[1] * s[c][1] + v[2] * s[c][2]
                    into[at : at + NEWS, lanes(c, e)] = q.reshape(NEWS, LANES)

    def build_new(t, group, into):
        for e in range(2):
            for k in range(NGROUP):
                s = [[spread(t, a, b, e, HELD + group * NGROUP + k) for b in range(3)] for a in range(3)]
                for r in range(0, TOTAL, NTILE):
                    v = [vall[t, e * 3 + b, r : r + NTILE].reshape(NTILE // 16, 16, LANES) for b in range(3)]
                    for c in range(3):
                        q = v[0] * s[c][0] + v[1] * s[c][1] + v[2] * s[c][2]
                        into[k * TOTAL + r : k * TOTAL + r + NTILE, lanes(c, e)] = q.reshape(NTILE, LANES)

    acc_h[...] = jnp.zeros_like(acc_h)
    acc_a[...] = jnp.zeros_like(acc_a)
    slopes_inner(1, 0)
    slopes_inner(1, 1)
    leave(SENDS[1]).start()
    slopes_inner(2, 0)
    slopes_inner(2, 1)
    landed(0)
    landed(1)
    whole(0)
    build_held(0, 0, left)
    build_held(0, 1, left)
    whole(1)

    def tick(t, following, now, then):
        for half in range(2):
            build_held(following, half, then)
            acc_h[half] += contract(t, now[half * 2 * HCOLS : (half + 1) * 2 * HCOLS])

    def before1():
        landed(3)
        landed(2)
        whole(2)

    def before2():
        landed(4)
        halo(0).start()
        shared(3)
        halo(0).wait_recv()
        slopes_outer(0)
        whole(3)

    def before3():
        landed(6)
        shared(4)
        landed(7)
        halo(1).start()
        whole(4)

    def before4():
        landed(5)
        shared(6)
        whole(5)

    def before5():
        halo(1).wait_recv()
        slopes_outer(1)
        shared(7)
        whole(6)

    def ticks(i, carry):
        pl.when(i == 1)(before2)
        pl.when(i == 2)(before4)
        pl.when(i == 3)(lambda: whole(7))
        tick(2 * i, 2 * i + 1, left, right)
        pl.when(i == 0)(before1)
        pl.when(i == 1)(before3)
        pl.when(i == 2)(before5)
        tick(2 * i + 1, jnp.minimum(2 * i + 2, CHUNKS - 1), right, left)
        return carry

    lax.fori_loop(0, CHUNKS // 2, ticks, 0)

    class Job:
        def __init__(self, n, bufs, width, source, maps, sinks):
            self.n, self.width, self.source, self.maps, self.sinks = n, width, source, maps, sinks
            self.f, self.s1, self.r1, self.t1, self.s2, self.r2, self.t2, self.r3 = bufs

        def first(self):
            for e in range(2):
                for p in range(4):
                    for q in range(4):
                        at = (q * 4 + p) if e == 0 else (p * 4 + q)
                        rows = [self.maps[e](2 * at + z) for z in range(2)]
                        for z in range(2):
                            self.f[e, p, q * 16 + z * 8 : q * 16 + z * 8 + 8, :] = self.source(e, rows[z])
                        self.s1[e, p, q * 16 : q * 16 + 16, :] = self.f[e, p, q * 16 : q * 16 + 16, :].astype(BF16)
            for copy in self.copies1():
                copy.start()

        def copies1(self):
            found = []
            for d in (1, 2, 3):
                for e in range(2):
                    p = ((px if e == 0 else py) + d) % 4
                    found.append(
                        remote(
                            self.s1.at[e, p], self.r1.at[e, d - 1],
                            rs1_send.at[self.n, e, d - 1], rs1_recv.at[self.n, e, d - 1],
                            (along_x if e == 0 else along_y)[d - 1],
                        )
                    )
            return found

        def second(self):
            for copy in self.copies1():
                copy.wait()
            for e in range(2):
                p = px if e == 0 else py
                t = self.f[e, p]
                for d in range(3):
                    t = t + self.r1[e, d].astype(F32)
                for q in range(4):
                    self.t1[e, q] = t[q * 16 : q * 16 + 16]
                    self.s2[e, q] = t[q * 16 : q * 16 + 16].astype(BF16)
            for copy in self.copies2():
                copy.start()

        def copies2(self):
            found = []
            for d in (1, 2, 3):
                for e in range(2):
                    q = ((py if e == 0 else px) + d) % 4
                    found.append(
                        remote(
                            self.s2.at[e, q], self.r2.at[e, d - 1],
                            rs2_send.at[self.n, e, d - 1], rs2_recv.at[self.n, e, d - 1],
                            (along_y if e == 0 else along_x)[d - 1],
                        )
                    )
            return found

        def third(self):
            for copy in self.copies2():
                copy.wait()
            for e in range(2):
                t = self.t1[e, py if e == 0 else px]
                for d in range(3):
                    t = t + self.r2[e, d].astype(F32)
                self.t2[e, 0] = t[0:8]
                self.t2[e, 1] = t[8:16]
            for copy in self.copies3():
                copy.start()

        def copies3(self):
            return [
                remote(
                    self.t2.at[e, 1 - pz], self.r3.at[e],
                    rs3_send.at[self.n, e], rs3_recv.at[self.n, e], across,
                )
                for e in range(2)
            ]

        def last(self):
            for copy in self.copies3():
                copy.wait()
            for e in range(2):
                ref, at = self.sinks[e]
                found = self.arrange((self.t2[e, pz] + self.r3[e]) * WEIGHT)
                ref[:, at : at + self.width] = found[: ref.shape[0]]

        def arrange(self, found):
            if self.n < 2:
                return found
            pieces = []
            for k in range(0, self.width, TOTAL):
                starts = range(k, k + TOTAL, ROWS)
                pieces += [found[:, i : i + HELD] for i in starts]
                pieces += [found[:, i + HELD : i + ROWS] for i in starts]
            return jnp.concatenate(pieces, 1)

    def held_job(half):
        def source(e, row):
            return acc_h[half, row : row + 8, e * HCOLS : (e + 1) * HCOLS]

        bufs = [b.at[half] for b in (f_h, s1_h, r1_h, t1_h, s2_h, r2_h, t2_h, r3_h)]
        return Job(half, bufs, HCOLS, source, (row_every, row_held),
                   ((out_w, half * HCOLS), (out_q, half * HCOLS)))

    def new_job(group):
        width = ACOLS // 2

        def source(e, row):
            return acc_a[group, row : row + 8, e * width : (e + 1) * width]

        bufs = [b.at[group] for b in (f_a, s1_a, r1_a, t1_a, s2_a, r2_a, t2_a, r3_a)]
        return Job(2 + group, bufs, width, source, (row_every, row_every),
                   ((out_a, group * ACOLS), (out_a, group * ACOLS + width)))

    jobs = [held_job(0), held_job(1), new_job(0), new_job(1)]
    jobs[0].first()
    jobs[1].first()

    one, two = left.at[0:ACOLS], right.at[0:ACOLS]

    def pairs(group):
        def pair(i, carry):
            build_new(2 * i + 1, group, two)
            acc_a[group] += contract(2 * i, one[...])
            build_new(jnp.minimum(2 * i + 2, CHUNKS - 1), group, one)
            acc_a[group] += contract(2 * i + 1, two[...])
            return carry

        build_new(0, group, one)
        lax.fori_loop(0, CHUNKS // 2, pair, 0)

    pairs(0)
    jobs[2].first()
    jobs[0].second()
    pairs(1)
    jobs[3].first()
    jobs[1].second()
    jobs[0].third()
    jobs[2].second()
    jobs[1].third()
    jobs[0].last()
    jobs[2].third()
    jobs[3].second()
    jobs[1].last()
    jobs[2].last()
    jobs[3].third()
    jobs[3].last()
    for t in range(CHUNKS):
        if t in RELAYED:
            onward(t).wait_send()
        to_core(t).wait_send()
        pass_on(t).wait_send()
    halo(0).wait_send()
    halo(1).wait_send()


def rs_scratch(lead, width):
    return [
        pltpu.VMEM(lead + (2, 4, 64, width), F32),
        pltpu.VMEM(lead + (2, 4, 64, width), BF16),
        pltpu.VMEM(lead + (2, 3, 64, width), BF16),
        pltpu.VMEM(lead + (2, 4, 16, width), F32),
        pltpu.VMEM(lead + (2, 4, 16, width), BF16),
        pltpu.VMEM(lead + (2, 3, 16, width), BF16),
        pltpu.VMEM(lead + (2, 2, 8, width), F32),
        pltpu.VMEM(lead + (2, 8, width), F32),
    ]


def per_device(held_modes, new_modes):
    own = jnp.concatenate([held_modes, new_modes], 0)
    own = own.transpose(2, 3, 1, 0, 4).reshape(CHUNKS, PARTS, ROWS, LANES)
    vmem = pl.BlockSpec(memory_space=pltpu.VMEM)
    dma = pltpu.SemaphoreType.DMA
    out_a, out_w, out_q = pl.pallas_call(
        kernel,
        out_shape=(
            jax.ShapeDtypeStruct((8, 2 * ACOLS), F32),
            jax.ShapeDtypeStruct((8, 2 * HCOLS), F32),
            jax.ShapeDtypeStruct((7, 2 * HCOLS), F32),
        ),
        in_specs=[pl.BlockSpec(memory_space=pl.ANY)],
        out_specs=(vmem, vmem, vmem),
        scratch_shapes=[
            pltpu.VMEM((CHUNKS, PARTS, ROWS, LANES), BF16),
            pltpu.VMEM((6, PARTS, ROWS, LANES), BF16),
            pltpu.VMEM((CHUNKS, PARTS, TOTAL, LANES), BF16),
            pltpu.VMEM((CHUNKS, PARTS, NEWS, LANES), BF16),
            pltpu.VMEM((CHUNKS, 9, 2, ROWS, LANES), F32),
            pltpu.VMEM((4 * HCOLS, DEPTH), BF16),
            pltpu.VMEM((4 * HCOLS, DEPTH), BF16),
            pltpu.VMEM((2, TOTAL, 2 * HCOLS), F32),
            pltpu.VMEM((2, TOTAL, ACOLS), F32),
            *rs_scratch((2,), HCOLS),
            *rs_scratch((2,), ACOLS // 2),
            *[dma((CHUNKS,))] * 8,
            dma((2,)),
            dma((2,)),
            dma((CHUNKS,)),
            dma((CHUNKS,)),
            dma((4, 2, 3)),
            dma((4, 2, 3)),
            dma((4, 2, 3)),
            dma((4, 2, 3)),
            dma((4, 2)),
            dma((4, 2)),
        ],
        compiler_params=pltpu.CompilerParams(
            collective_id=0, has_side_effects=True, vmem_limit_bytes=60 * 2**20
        ),
        cost_estimate=pl.CostEstimate(
            flops=2 * 5632 * TOTAL * CHUNKS * DEPTH, bytes_accessed=2**20, transcendentals=0
        ),
    )(own)
    return (out_a, out_w, out_q)


def solution(mesh):
    placed = (P("mode", None, "grid", None, None), P("mode", None, "grid", None, None))
    return jax.shard_map(
        per_device,
        mesh=mesh,
        in_specs=placed,
        out_specs=(P("grid", "mode"), P("grid", "mode"), P("grid", "mode")),
        check_vma=False,
    )
```

time: 95.6 us -> 87.5 us (0.915)
  Pallas kernels: 87.8 us -> 80.9 us
  local copies, waits for them, and re-layouts: 5.15 us -> 4.05 us
    pallas_call x1, Pallas kernels: 87.8 us -> 80.9 us  [per_device(): pl.pallas_call(kernel, out_shape=(jax.ShapeDtypeStruct((8, 2 * ACOLS), F3...]
    unnamed x6 -> x7, local copies, waits for them, and re-layouts: 1.25 us -> 2.96 us
    transpose x0 -> x1, other arithmetic: none -> 1.67 us  [per_device(): own = own.transpose(2, 3, 1, 0, 4).reshape(CHUNKS, PARTS, ROWS, LANES)]
    concatenate x2 -> x0, other arithmetic: 1.67 us -> none  [the longest x1 0.96 us: per_device(): jnp.concatenate([held_modes.transpose(2, 0, 1, 3, 4).reshape(PLANES, HELD...]
    reshape x6 -> x0, local copies, waits for them, and re-layouts: 1.51 us -> none  [the longest x1 0.99 us: per_device(): by_mode = out_a.reshape(8, NEW, 4, ROWS)]
    transpose x2 -> x1, local copies, waits for them, and re-layouts: 2.26 us -> 1.1 us  [per_device(): own = own.transpose(2, 3, 1, 0, 4).reshape(CHUNKS, PARTS, ROWS, LANES)]
where the time goes in v2:
time: 87.5 us; the launch traced here: 87.3 us
  Pallas kernels  80.9 us (92%)
  local copies, waits for them, and re-layouts  4.05 us (5%)
  other arithmetic  1.67 us (2%)
    pallas_call x1, Pallas kernels, per_device(): pl.pallas_call(kernel, out_shape=(jax.ShapeDtypeStruct((8, 2 * ACOLS), F3...  80.9 us
    unnamed x7, local copies, waits for them, and re-layouts  2.96 us

profile of v2, /device:TPU:0, one launch (start us, length us, event | category | flops | bytes accessed | tf_op | source)
XLA Modules:
  0.0 87.3 jit_solution(17030862240104666557)
XLA Ops:
  0.6 1.7 %maximum_bitcast_fusion = bf16[4,4,3,64,128]{4,1,0,2,3:T(4,128)(2,1)S(1)} fusion(bf16[8,3,4,4,128]{4,3,2,1,0:T(4,128)(2,1)} %param.3, bf16[56,3,4,4,128]{4,3,2,1,0:T(4,128)(2,1)} %param.2), kind=kLoop, calls=%fused_computation | loop fusion | flops 393216 | bytes 1572864 | tf_op jit(solution)/shard_map/transpose | solution.py:442
  2.3 1.1 %copy.5 = bf16[4,4,3,64,128]{4,3,2,1,0:T(8,128)(2,1)} copy(bf16[4,4,3,64,128]{4,1,0,2,3:T(4,128)(2,1)S(1)} %maximum_bitcast_fusion) | data formatting | bytes 1572864 | tf_op jit(solution)/shard_map/transpose | solution.py:442
  3.4 80.9 %shard_map.49 = (f32[8,2048]{1,0:T(8,128)}, f32[8,1792]{1,0:T(8,128)}, f32[7,1792]{1,0:T(8,128)}) custom-call(bf16[8,6,64,128]{3,2,1,0:T(8,128)(2,1)} %bitcast.3), custom_call_target="tpu_custom_call" | custom-call | flops 17716740096 | bytes 1048576 | tf_op jit(solution)/shard_map/pallas_call | solution.py:445
  84.3 0.0 copy-start.1
  84.3 1.5 %copy.9 = f32[8,2048]{1,0:T(8,128)} copy(f32[8,2048]{1,0:T(8,128)} %get-tuple-element.6) | data formatting | bytes 131072
  85.8 0.0 copy-done.1
  85.8 0.0 copy-start
  85.8 0.6 copy.10
  86.4 0.2 copy-done
  86.6 0.6 copy.11
Async XLA Ops:
  84.3 1.5 %copy-start.1 = (f32[8,1792]{1,0:T(8,128)S(1)}, f32[8,1792]{1,0:T(8,128)}, u32[]{:S(2)}) copy-start(f32[8,1792]{1,0:T(8,128)} %get-tuple-element.7) | copy-start | bytes 172036
  85.8 0.8 copy-start

commit v3 on v2

--- a/solution.py
+++ b/solution.py
@@ -351,8 +351,8 @@
                 copy.wait()
             for e in range(2):
                 ref, at = self.sinks[e]
-                found = self.arrange((self.t2[e, pz] + self.r3[e]) * WEIGHT)
-                ref[:, at : at + self.width] = found[: ref.shape[0]]
+                found = self.arrange(self.t2[e, pz] + self.r3[e])
+                ref[:, at : at + self.width] = found
 
         def arrange(self, found):
             if self.n < 2:
@@ -447,7 +447,7 @@
         out_shape=(
             jax.ShapeDtypeStruct((8, 2 * ACOLS), F32),
             jax.ShapeDtypeStruct((8, 2 * HCOLS), F32),
-            jax.ShapeDtypeStruct((7, 2 * HCOLS), F32),
+            jax.ShapeDtypeStruct((8, 2 * HCOLS), F32),
         ),
         in_specs=[pl.BlockSpec(memory_space=pl.ANY)],
         out_specs=(vmem, vmem, vmem),
@@ -482,7 +482,7 @@
             flops=2 * 5632 * TOTAL * CHUNKS * DEPTH, bytes_accessed=2**20, transcendentals=0
         ),
     )(own)
-    return (out_a, out_w, out_q)
+    return (out_a * WEIGHT, out_w * WEIGHT, out_q[:7] * WEIGHT)
 
 
 def solution(mesh):

time: 87.5 us -> 87.5 us (level)
  other arithmetic: 1.67 us -> 4.42 us
  local copies, waits for them, and re-layouts: 4.05 us -> 1.31 us
    mul x0 -> x3, other arithmetic: none -> 2.75 us  [per_device(): return (out_a * WEIGHT, out_w * WEIGHT, out_q[:7] * WEIGHT)]
    unnamed x7 -> x4, local copies, waits for them, and re-layouts: 2.96 us -> 0.22 us
where the time goes in v3:
time: 87.5 us; the launch traced here: 87.3 us
  Pallas kernels  80.9 us (92%)
  other arithmetic  4.42 us (5%)
  local copies, waits for them, and re-layouts  1.31 us (1%)
    pallas_call x1, Pallas kernels, per_device(): pl.pallas_call(kernel, out_shape=(jax.ShapeDtypeStruct((8, 2 * ACOLS), F3...  80.9 us
    mul x3, other arithmetic, per_device(): return (out_a * WEIGHT, out_w * WEIGHT, out_q[:7] * WEIGHT)  2.75 us

profile of v3, /device:TPU:0, one launch (start us, length us, event | category | flops | bytes accessed | tf_op | source)
XLA Modules:
  0.0 87.3 jit_solution(15277517063184737235)
XLA Ops:
  0.6 1.7 %maximum_bitcast_fusion = bf16[4,4,3,64,128]{4,1,0,2,3:T(4,128)(2,1)S(1)} fusion(bf16[8,3,4,4,128]{4,3,2,1,0:T(4,128)(2,1)} %param.3, bf16[56,3,4,4,128]{4,3,2,1,0:T(4,128)(2,1)} %param.2), kind=kLoop, calls=%fused_computation | loop fusion | flops 393216 | bytes 1572864 | tf_op jit(solution)/shard_map/transpose | solution.py:442
  2.3 1.1 %copy.5 = bf16[4,4,3,64,128]{4,3,2,1,0:T(8,128)(2,1)} copy(bf16[4,4,3,64,128]{4,1,0,2,3:T(4,128)(2,1)S(1)} %maximum_bitcast_fusion) | data formatting | bytes 1572864 | tf_op jit(solution)/shard_map/transpose | solution.py:442
  3.4 80.9 %shard_map.49 = (f32[8,2048]{1,0:T(8,128)}, f32[8,1792]{1,0:T(8,128)}, f32[8,1792]{1,0:T(8,128)}) custom-call(bf16[8,6,64,128]{3,2,1,0:T(8,128)(2,1)} %bitcast.3), custom_call_target="tpu_custom_call" | custom-call | flops 17716740096 | bytes 1048576 | tf_op jit(solution)/shard_map/pallas_call | solution.py:445
  84.3 0.0 copy-start.1
  84.3 1.5 %broadcast_multiply_fusion = f32[8,2048]{1,0:T(8,128)} fusion(f32[8,2048]{1,0:T(8,128)} %get-tuple-element.6), kind=kLoop, calls=%fused_computation.2 | loop fusion | flops 16384 | bytes 131072 | tf_op jit(solution)/shard_map/mul | solution.py:485
  85.8 0.0 copy-done.1
  85.8 0.0 copy-start
  85.8 0.6 broadcast_multiply_fusion.1
  86.4 0.2 copy-done
  86.6 0.6 slice_multiply_fusion
Async XLA Ops:
  84.3 1.5 %copy-start.1 = (f32[8,1792]{1,0:T(8,128)S(1)}, f32[8,1792]{1,0:T(8,128)}, u32[]{:S(2)}) copy-start(f32[8,1792]{1,0:T(8,128)} %get-tuple-element.7) | copy-start | bytes 172036
  85.8 0.8 copy-start
